TPU v7x, 256 devices: a whole 4x4x8 slice. The times are simulated.
256 devices in a mesh: section: 8 (over z), expert: 32 (over x, y, core).
Axes of the slice: x: 4, y: 4, z: 8, core: 2. Of those that a mesh axis runs over, the one named last changes fastest.
Arguments:
- residual: bfloat16 [4096, 3584], P(('section', 'expert')), may hold values from -6 to 6
- query_latent: bfloat16 [4096, 65536], P(('section', 'expert')), may hold values from -64 to 64
- query_rotary: bfloat16 [4096, 8192], P(('section', 'expert')), may hold values from -64 to 64
- cache_latent: bfloat16 [1024, 512, 512], P(('section', 'expert')), may hold values from -8 to 8
- cache_rotary: bfloat16 [1024, 64, 512], P(('section', 'expert')), may hold values from -8 to 8
- new_latent: bfloat16 [4096, 512], P(('section', 'expert')), may hold values from -6 to 6
- new_rotary: bfloat16 [64, 4096], P(None, ('section', 'expert')), may hold values from -6 to 6
- cache_len: int32 [1024], P(('section', 'expert')), may hold values from 128 to 512, as said below
- route_ids: int32 [4096, 2], P('section'), may hold values from 0 to 3, all different within a row; in each aligned block of 16 rows (0 to 15, 16 to 31, ...) at most 12 rows name the same one
- routing_weight: float32 [4096, 2], P('section'), may hold values from 0.1 to 1
- norm_gain: float32 [8, 3584], P('section'), may hold values from 0.5 to 1.5
- value_up_matrix: bfloat16 [8, 128, 512, 128], P('section', 'expert'), may hold values from -0.25 to 0.25
- out_weight: bfloat16 [8, 16384, 3584], P('section', 'expert'), may hold values from -0.1875 to 0.1875
- gate_weight: bfloat16 [8, 3584, 8192], P('section', None, 'expert'), may hold values from -0.09375 to 0.09375
- up_weight: bfloat16 [8, 3584, 8192], P('section', None, 'expert'), may hold values from -0.09375 to 0.09375
- down_weight: bfloat16 [8, 8192, 3584], P('section', 'expert'), may hold values from -0.125 to 0.125
Outputs:
- handed: bfloat16 [4096, 3584], P(('section', 'expert'))
Inputs may be any that keep to these rules, and one draw needn't show every extreme that they name: `route_ids`: each row names 2 different experts; among the rows of one device no expert is named more than 12 times, and some expert reaches 12. `cache_len`: at least one sequence holds exactly 512 cached tokens.
All inputs are finite; a program needn't handle non-finite values.
Results may differ from a plain program's by a relative error of at most 0.0065.
Values may be sent and summed in bfloat16 or wider, within the bound.
A program may use at most 128 MiB of HBM per device.

v0:
```python
import jax
import jax.numpy as jnp
from jax import lax
from jax.sharding import PartitionSpec as P

KVL = 512
ROPE = 64
VDIM = 128
EXPERTS = 4
TOPK = 2
CAP = 12


def passed_along(value, axis, steps):
    count = lax.axis_size(axis)
    pairs = [(source, (source + steps) % count) for source in range(count)]
    return lax.ppermute(value, axis, pairs)


def attend_latent_heads(
    query_latent, query_rotary, cache_latent, cache_rotary, new_latent, new_rotary, length
):
    block_len = query_latent.shape[0]
    head_count = query_latent.shape[1]
    keys_all = jnp.concatenate([cache_latent, new_latent], axis=0)
    rotary_all = jnp.concatenate([cache_rotary, new_rotary], axis=1)
    flat_latent = query_latent.reshape(block_len * head_count, query_latent.shape[2])
    flat_rotary = query_rotary.reshape(block_len * head_count, query_rotary.shape[2])
    scores = jnp.dot(flat_latent, keys_all.T, preferred_element_type=jnp.float32)
    scores = scores + jnp.dot(flat_rotary, rotary_all, preferred_element_type=jnp.float32)
    scores = scores * (VDIM + ROPE) ** (-0.5)
    cached = cache_latent.shape[0]
    position = jnp.arange(cached + block_len, dtype=jnp.int32)[None, :]
    token_pos = (jnp.arange(block_len * head_count, dtype=jnp.int32) // head_count)[:, None]
    visible = jnp.where(position < cached, position < length, position - cached <= token_pos)
    scores = jnp.where(visible, scores, -1e30)
    largest = jnp.max(scores, axis=1, keepdims=True)
    exponents = jnp.exp(scores - largest)
    probability = (exponents / jnp.sum(exponents, axis=1, keepdims=True)).astype(jnp.bfloat16)
    context_vectors = jnp.dot(probability, keys_all, preferred_element_type=jnp.float32).astype(
        jnp.bfloat16
    )
    return context_vectors.reshape(block_len, head_count, keys_all.shape[1])


def expert_slice(rows_in, gate_cols, up_cols, down_rows):
    gate_val = jnp.dot(rows_in, gate_cols, preferred_element_type=jnp.float32)
    up_val = jnp.dot(rows_in, up_cols, preferred_element_type=jnp.float32)
    activation_value = (jax.nn.silu(gate_val) * up_val).astype(jnp.bfloat16)
    return jnp.dot(activation_value, down_rows, preferred_element_type=jnp.float32)


def local(
    residual,
    query_latent,
    query_rotary,
    cache_latent,
    cache_rotary,
    new_latent,
    new_rotary,
    cache_len,
    route_ids,
    routing_weight,
    norm_gain,
    value_up_matrix,
    out_weight,
    gate_weight,
    up_weight,
    down_weight,
):
    row_count, model_width = residual.shape
    sequences = cache_len.shape[0]
    block_len = row_count // sequences
    head_count = query_latent.shape[1] // KVL
    lat_query = query_latent.reshape(sequences, block_len, head_count, KVL)
    rot_query = query_rotary.reshape(sequences, block_len, head_count, ROPE)
    lat_new = new_latent.reshape(sequences, block_len, KVL)
    rot_new = new_rotary.reshape(ROPE, sequences, block_len).transpose(1, 0, 2)
    context_vectors = jax.vmap(attend_latent_heads)(
        lat_query, rot_query, cache_latent, cache_rotary, lat_new, rot_new, cache_len
    )
    context_vectors = context_vectors.reshape(row_count, head_count, KVL)
    split_by_head = lax.all_to_all(
        context_vectors, "expert", split_axis=1, concat_axis=0, tiled=True
    )
    head_output = jnp.einsum(
        "cio,iop->cip", split_by_head, value_up_matrix[0], preferred_element_type=jnp.float32
    ).astype(jnp.bfloat16)
    flat_heads = head_output.reshape(head_output.shape[0], -1)
    attention = lax.psum_scatter(
        jnp.dot(flat_heads, out_weight[0], preferred_element_type=jnp.float32),
        "expert",
        scatter_dimension=0,
        tiled=True,
    )
    hidden = residual.astype(jnp.float32) + attention
    normed = (
        hidden
        * lax.rsqrt(jnp.mean(hidden * hidden, axis=1, keepdims=True) + 1e-06)
        * norm_gain[0][None, :]
    ).astype(jnp.bfloat16)
    devices = lax.axis_size("expert")
    my_index = lax.axis_index("expert")
    group_size = devices // EXPERTS
    own_ids = lax.dynamic_slice_in_dim(route_ids, my_index * row_count, row_count, 0).reshape(-1)
    own_weight = lax.dynamic_slice_in_dim(
        routing_weight, my_index * row_count, row_count, 0
    ).reshape(-1)
    picks = (own_ids[:, None] == jnp.arange(EXPERTS, dtype=jnp.int32)[None, :]).astype(jnp.int32)
    earlier = jnp.cumsum(picks, axis=0) - picks
    slot_index = jnp.sum(earlier * picks, axis=1)
    target = own_ids * CAP + slot_index
    chooser = (jnp.arange(EXPERTS * CAP, dtype=jnp.int32)[:, None] == target[None, :]).astype(
        jnp.float32
    )
    owner_of = (
        jnp.arange(row_count * TOPK, dtype=jnp.int32)[:, None] // TOPK
        == jnp.arange(row_count, dtype=jnp.int32)[None, :]
    ).astype(jnp.float32)
    placement = jnp.dot(chooser, owner_of, precision=lax.Precision.HIGHEST)
    packed = jnp.dot(
        placement.astype(jnp.bfloat16), normed, preferred_element_type=jnp.float32
    ).astype(jnp.bfloat16)
    outgoing = jnp.repeat(packed.reshape(EXPERTS, CAP, model_width), group_size, axis=0)
    incoming = lax.all_to_all(outgoing, "expert", split_axis=0, concat_axis=0, tiled=True)
    item_count = incoming.shape[1]
    flat_in = incoming.reshape(-1, model_width)
    partial_value = expert_slice(flat_in, gate_weight[0], up_weight[0], down_weight[0])
    partial_value = partial_value.reshape(devices, item_count, model_width)
    returned = lax.all_to_all(
        partial_value.astype(jnp.bfloat16), "expert", split_axis=0, concat_axis=0, tiled=True
    ).astype(partial_value.dtype)
    summed = (
        returned.reshape(EXPERTS, group_size, CAP, model_width)
        .sum(axis=1)
        .reshape(EXPERTS * CAP, model_width)
    )
    combine_map = jnp.dot(
        owner_of.T * own_weight[None, :], chooser.T, precision=lax.Precision.HIGHEST
    )
    expert_mix = jnp.dot(combine_map, summed, precision=lax.Precision.HIGHEST)
    layer_out = (hidden + expert_mix).astype(jnp.bfloat16)
    return passed_along(layer_out, "section", 1)


def solution(mesh):
    placed = (
        P(("section", "expert"), None),
        P(("section", "expert"), None),
        P(("section", "expert"), None),
        P(("section", "expert"), None, None),
        P(("section", "expert"), None, None),
        P(("section", "expert"), None),
        P(None, ("section", "expert")),
        P(("section", "expert")),
        P("section", None),
        P("section", None),
        P("section", None),
        P("section", "expert", None, None),
        P("section", "expert", None),
        P("section", None, "expert"),
        P("section", None, "expert"),
        P("section", "expert", None),
    )
    return jax.shard_map(
        local, mesh=mesh, in_specs=placed, out_specs=P(("section", "expert"), None), check_vma=False
    )
```

profile of v0, /device:TPU:8, one launch (start us, length us, event | category | flops | bytes accessed | tf_op | source)
XLA Modules:
  0.0 306.9 jit_solution(14578734581769670503)
XLA Ops:
  6.6 3.2 %constant_dynamic-update-slice_fusion.1 = bf16[4,516,512]{2,1,0:T(8,128)(2,1)} fusion(bf16[4,512,512]{2,1,0:T(8,128)(2,1)} %param.19), kind=kLoop, calls=%fused_computation.48 | loop fusion | bytes 4194304
  9.8 0.5 reshape_reshape.7
  10.4 0.1 copy.30
  10.5 3.2 %reshape_reshape.6 = bf16[4,512,512]{2,1,0:T(8,128)(2,1)} reshape(bf16[16,65536]{1,0:T(8,128)(2,1)} %param.17) | data formatting | bytes 4194304 | tf_op jit(solution)/shard_map/vmap()/reshape;reshape | solution.py:27
  13.8 0.6 constant_dynamic-update-slice_fusion
  14.5 0.2 broadcast_compare_fusion
  14.7 0.8 fusion.19
  15.5 0.7 copy-done.2
  16.2 1.8 bitcast_select_fusion
  18.0 2.0 copy-done.1
  19.9 0.8 fusion.41
  20.8 7.4 %fusion.6 = bf16[4,512,512]{2,1,0:T(8,128)(2,1)} fusion(bf16[4,516,512]{2,1,0:T(8,128)(2,1)} %constant_dynamic-update-slice_fusion, f32[4,512]{1,0:T(4,128)S(1)} %fusion.41, f32[4,512,516]{1,2,0:T(8,128)} %copy-done.1), kind=kOutput, calls=%fused_computation.13 | convolution fusion | flops 1086351872 | bytes 8445952 | tf_op jit(solution)/shard_map/vmap()/dot_general | solution.py:40
  28.2 2.8 copy.32
  31.0 34.1 %all_to_all.28 = bf16[16,128,512]{2,0,1:T(8,128)(2,1)S(1)} all-to-all(bf16[16,128,512]{2,0,1:T(8,128)(2,1)S(1)} %copy.32), channel_id=1, replica_groups=mesh['section'=8,'expert'=32] {'expert'}, dimensions={1} | all-to-all | bytes 4194304 | tf_op jit(solution)/shard_map/all_to_all | solution.py:83
  65.1 0.2 copy.33
  65.3 0.8 copy-done.7
  66.1 0.8 convolution_convert_fusion.2
  66.9 0.3 copy-done.4
  67.3 5.1 %fusion.2 = f32[512,3584]{1,0:T(8,128)} fusion(bf16[512,512]{0,1:T(8,128)(2,1)S(1)} %bitcast.53, bf16[1,512,3584]{2,1,0:T(8,128)(2,1)S(1)} %copy-done.4), kind=kOutput, calls=%fused_computation.9 | convolution fusion | flops 1879048192 | bytes 11534336 | tf_op jit(solution)/shard_map/dot_general | solution.py:91
  72.4 0.8 constant_dynamic-slice_fusion
  73.2 0.1 copy.36
  73.3 0.1 reshape.139
  73.5 0.2 select_reduce_fusion
  73.7 0.2 convolution_convert_fusion.3
  74.0 95.0 %reduce-scatter.2.cloned.1.call-done = f32[16,3584]{1,0:T(8,128)} async-done(((f32[512,3584]{1,0:T(8,128)}), f32[16,3584]{1,0:T(8,128)}) %reduce-scatter.2.cloned.1.call-update) | async-done | bytes 229392 | tf_op jit(solution)/shard_map/reduce_scatter | solution.py:90
  169.0 1.1 multiply_reduce_fusion
  170.1 1.2 convolution_convert_fusion.1
  171.3 0.1 reshape.140
  171.4 0.4 broadcast_in_dim.43
  171.8 49.6 %all_to_all.29 = bf16[32,12,3584]{2,1,0:T(8,128)(2,1)} all-to-all(bf16[32,12,3584]{2,1,0:T(8,128)(2,1)S(1)} %bitcast.49), channel_id=1, replica_groups=mesh['section'=8,'expert'=32] {'expert'}, dimensions={0} | all-to-all | bytes 5505024 | tf_op jit(solution)/shard_map/all_to_all | solution.py:125
  221.4 5.4 %reshape.142 = bf16[384,3584]{1,0:T(8,128)(2,1)} reshape(bf16[32,12,3584]{2,1,0:T(8,128)(2,1)} %all_to_all.29) | data formatting | bytes 5505024 | tf_op jit(solution)/shard_map/reshape | solution.py:127
  226.7 3.3 %fusion.10 = f32[384,256]{1,0:T(8,128)S(1)} fusion(bf16[384,3584]{1,0:T(8,128)(2,1)} %reshape.142, bf16[1,3584,256]{2,1,0:T(8,128)(2,1)} %param.29), kind=kOutput, calls=%fused_computation.17 | convolution fusion | flops 704643072 | bytes 4980736 | tf_op jit(solution)/shard_map/dot_general | solution.py:47
  230.1 0.3 copy-done.14
  230.4 0.9 fusion.15
  231.4 0.9 convolution_convert_fusion
  232.3 3.4 %copy.38 = bf16[32,12,3584]{2,1,0:T(8,128)(2,1)} copy(bf16[32,12,3584]{2,0,1:T(8,128)(2,1)S(1)} %convolution_convert_fusion) | data formatting | bytes 5505024 | tf_op jit(solution)/shard_map/convert_element_type | solution.py:131
  235.7 5.7 %all-to-all-start.2 = ((bf16[32,12,3584]{2,1,0:T(8,128)(2,1)}), bf16[32,12,3584]{2,1,0:T(8,128)(2,1)}, u32[]{:S(2)}, u32[]{:S(2)}) async-start(bf16[32,12,3584]{2,1,0:T(8,128)(2,1)} %copy.38), calls=%async_computation.3 | async-start | bytes 7340032 | tf_op jit(solution)/shard_map/all_to_all | solution.py:130
  241.4 0.8 constant_dynamic-slice_fusion.1
  242.1 0.1 copy.35
  242.2 0.1 mul.68
  242.3 0.8 fusion.26
  243.1 45.8 %all-to-all-done.2 = bf16[32,12,3584]{2,1,0:T(8,128)(2,1)} async-done(((bf16[32,12,3584]{2,1,0:T(8,128)(2,1)}), bf16[32,12,3584]{2,1,0:T(8,128)(2,1)}, u32[]{:S(2)}, u32[]{:S(2)}) %all-to-all-start.2) | async-done | bytes 2752544 | tf_op jit(solution)/shard_map/all_to_all | solution.py:130
  288.8 2.7 convert_reduce_fusion
  291.6 0.1 reshape.145
  291.7 1.4 fusion.1
  293.1 1.6 collective-permute-start
  294.7 4.7 %collective-permute-done = bf16[16,3584]{1,0:T(8,128)(2,1)S(1)} collective-permute-done((bf16[16,3584]{1,0:T(8,128)(2,1)S(1)}, bf16[16,3584]{1,0:T(8,128)(2,1)S(1)}, u32[]{:S(2)}, u32[]{:S(2)}) %collective-permute-start) | collective-permute-done | bytes 114720 | tf_op jit(solution)/shard_map/ppermute | solution.py:17
  299.4 0.6 copy.48
  (38 shorter events, 0.4 us)
Async XLA Ops:
  6.5 224.8 %copy-start = (bf16[1,256,3584]{2,1,0:T(8,128)(2,1)S(1)}, bf16[1,256,3584]{2,1,0:T(8,128)(2,1)}, u32[]{:S(2)}) copy-start(bf16[1,256,3584]{2,1,0:T(8,128)(2,1)} %param.31) | copy-start | bytes 5505028
  6.5 3.3 %copy-start.10 = (bf16[16,512]{1,0:T(8,128)(2,1)S(1)}, bf16[16,512]{1,0:T(8,128)(2,1)}, u32[]{:S(2)}) copy-start(bf16[16,512]{1,0:T(8,128)(2,1)} %param.21) | copy-start | bytes 49156
  6.5 3.3 %copy-start.8 = (bf16[16,8192]{1,0:T(8,128)(2,1)S(1)}, bf16[16,8192]{1,0:T(8,128)(2,1)}, u32[]{:S(2)}) copy-start(bf16[16,8192]{1,0:T(8,128)(2,1)} %param.18) | copy-start | bytes 786436
  6.5 3.8 %copy-start.12 = (bf16[64,16]{0,1:T(8,128)(2,1)S(1)}, bf16[64,16]{0,1:T(8,128)(2,1)}, u32[]{:S(2)}) copy-start(bf16[64,16]{0,1:T(8,128)(2,1)} %param.22) | copy-start | bytes 6148
  6.5 162.4 %reduce-scatter.2.cloned.1.call-start = ((), (), s32[]{:S(2)}) async-start(), calls=%async_computation.4 | async-start | bytes 7569408 | tf_op jit(solution)/shard_map/reduce_scatter | solution.py:90
  9.8 4.0 %copy-start.13 = (s32[4]{0:T(128)S(1)}, s32[4]{0:T(128)}, u32[]{:S(2)}) copy-start(s32[4]{0:T(128)} %param.23) | copy-start | bytes 52
  9.8 4.9 %copy-start.9 = (bf16[4,64,512]{2,1,0:T(8,128)(2,1)S(1)}, bf16[4,64,512]{2,1,0:T(8,128)(2,1)}, u32[]{:S(2)}) copy-start(bf16[4,64,512]{2,1,0:T(8,128)(2,1)} %param.20) | copy-start | bytes 786436
  13.8 1.7 copy-start.3
  14.5 1.8 copy-start.2
  18.0 2.0 copy-start.1
  65.1 1.0 copy-start.7
  65.1 2.2 copy-start.4
  72.4 1.1 copy-start.11
  72.4 96.6 %copy-start.6 = (bf16[16,3584]{1,0:T(8,128)(2,1)S(1)}, bf16[16,3584]{1,0:T(8,128)(2,1)}, u32[]{:S(2)}) copy-start(bf16[16,3584]{1,0:T(8,128)(2,1)} %param.16) | copy-start | bytes 344068
  226.7 3.4 %copy-start.5 = (bf16[384,3584]{1,0:T(8,128)(2,1)S(1)}, bf16[384,3584]{1,0:T(8,128)(2,1)}, u32[]{:S(2)}) copy-start(bf16[384,3584]{1,0:T(8,128)(2,1)} %reshape.142) | copy-start | bytes 8257540
  226.7 3.7 %copy-start.14 = (bf16[1,3584,256]{2,1,0:T(8,128)(2,1)S(1)}, bf16[1,3584,256]{2,1,0:T(8,128)(2,1)}, u32[]{:S(2)}) copy-start(bf16[1,3584,256]{2,1,0:T(8,128)(2,1)} %param.30) | copy-start | bytes 5505028
  235.7 53.1 %all-to-all-start.2 = ((bf16[32,12,3584]{2,1,0:T(8,128)(2,1)}), bf16[32,12,3584]{2,1,0:T(8,128)(2,1)}, u32[]{:S(2)}, u32[]{:S(2)}) async-start(bf16[32,12,3584]{2,1,0:T(8,128)(2,1)} %copy.38), calls=%async_computation.3 | async-start | bytes 7340032 | tf_op jit(solution)/shard_map/all_to_all | solution.py:130
  293.1 6.3 %collective-permute-start = (bf16[16,3584]{1,0:T(8,128)(2,1)S(1)}, bf16[16,3584]{1,0:T(8,128)(2,1)S(1)}, u32[]{:S(2)}, u32[]{:S(2)}) collective-permute-start(bf16[16,3584]{1,0:T(8,128)(2,1)S(1)} %fusion.1), channel_id=1, source_target_pairs={{0,32},{32,64},{64,96},{96,128},{128,160},{160,192},{192,224},{224... | collective-permute-start | bytes 344072 | tf_op jit(solution)/shard_map/ppermute | solution.py:17
Sparse Core Ops, SparseCore 0:
  72.5 96.4 reduce-scatter.1
where the time goes:
time: 307 us
  waiting for transfers between devices  145 us (47%)
  blocking collectives  83.7 us (27%)
  local copies, waits for them, and re-layouts  26.8 us (9%)
  matrix products  24.6 us (8%)
  between operations  13.6 us (4%)
  starting transfers between devices  7.34 us (2%)
  other arithmetic  5.32 us (2%)
    reduce_scatter x1, waiting for transfers between devices, local(): lax.psum_scatter(jnp.dot(flat_heads, out_weight[0], preferred_element_typ...  95 us
    all_to_all x1, blocking collectives, local(): lax.all_to_all(outgoing, 'expert', split_axis=0, concat_axis=0, tiled=True)  49.6 us
    all_to_all x1, waiting for transfers between devices, local(): lax.all_to_all(partial_value.astype(jnp.bfloat16), 'expert', split_axis=0...  45.8 us
    all_to_all x1, blocking collectives, local(): lax.all_to_all(context_vectors, 'expert', split_axis=1, concat_axis=0, ti...  34.1 us
    unnamed x32, local copies, waits for them, and re-layouts  8.06 us
    dot_general x1, matrix products, attend_latent_heads(): jnp.dot(probability, keys_all, preferred_element_type=jnp.float32)  7.44 us
  transfers between devices with their start and end apart: 3, of which 3 were waited for; matrix products, arithmetic and copies ran while one was open for 1% of the time, Pallas kernels for 0%

commit v1 on v0

v1 whole, which is shorter than its diff:
```python
import jax
import jax.numpy as jnp
from jax import lax
from jax.experimental import pallas as pl
from jax.experimental.pallas import tpu as pltpu
from jax.sharding import PartitionSpec as P

D = 3584
KVL = 512
ROPE = 64
VDIM = 128
HEADS = 128
TB = 4
SEQ = 4
ROWS = 16
CACHE = 512
FF_DEV = 256
SIDE = 4
GROUP = 32
CHUNKS = 4
WIDE = D // CHUNKS
HALF = GROUP * ROWS // 2

BF16 = jnp.bfloat16
F32 = jnp.float32


def dot(a, b):
    return lax.dot_general(a, b, (((1,), (0,)), ((), ())), preferred_element_type=F32)


def dot_t(a, b):
    return lax.dot_general(a, b, (((1,), (1,)), ((), ())), preferred_element_type=F32)


def iota(shape, dim):
    return lax.broadcasted_iota(jnp.int32, shape, dim)


def layer_kernel(
    sections,
    residual_hbm,
    query_hbm,
    query_rot_hbm,
    latent_hbm,
    rotary_hbm,
    new_latent,
    new_rotary,
    cache_len,
    route_ids,
    routing_weight,
    norm_gain,
    value_up_hbm,
    out_weight_hbm,
    gate_hbm,
    up_hbm,
    down_hbm,
    out_hbm,
    residual,
    query,
    query_rot,
    latent,
    rotary,
    value_up,
    out_weight,
    gate_up,
    down,
    query_seq,
    rot_seq,
    keys_new,
    rot_new,
    context,
    arrived,
    diagonal,
    heads,
    chosen_all,
    chosen,
    cross_out,
    cross_in,
    first_out,
    first_in,
    second_out,
    second_in,
    hidden,
    gathered,
    hidden_units,
    activation,
    handed,
    load_sem,
    seq_sem,
    context_send,
    context_recv,
    sum_send,
    sum_recv,
    gather_send,
    gather_recv,
    hand_send,
    hand_recv,
):
    section = lax.axis_index("section")
    me = lax.axis_index("expert")
    core = me % 2
    chip = me // 2
    x = chip // SIDE
    y = chip % SIDE
    sibling = chip * 2 + 1 - core

    def device(chip_x, chip_y):
        return (chip_x * SIDE + chip_y) * 2 + core

    barrier = pltpu.get_barrier_semaphore()

    @pl.loop(1, GROUP)
    def _(offset):
        pl.semaphore_signal(barrier, inc=1, device_id={"expert": (me + offset) % GROUP})

    if sections > 1:
        pl.semaphore_signal(barrier, inc=1, device_id={"section": (section + 1) % sections})
        pl.semaphore_signal(
            barrier, inc=1, device_id={"section": (section + sections - 1) % sections}
        )

    loads = []

    def load(source, target, sem):
        copy = pltpu.make_async_copy(source, target, sem)
        copy.start()
        return copy

    load_query = load(query_hbm, query, load_sem.at[0])
    load_rot = load(query_rot_hbm, query_rot, load_sem.at[1])
    for b in range(SEQ):
        load(latent_hbm.at[b], latent.at[b], seq_sem.at[0, b])
        load(rotary_hbm.at[b], rotary.at[b], seq_sem.at[1, b])
    load_up = [
        load(value_up_hbm.at[0, j], value_up.at[:, pl.ds(j * VDIM, VDIM)], load_sem.at[2 + j])
        for j in range(4)
    ]
    load_out = load(out_weight_hbm.at[0], out_weight, load_sem.at[6])
    load_res = load(residual_hbm, residual, load_sem.at[7])
    load_gate = load(gate_hbm.at[0], gate_up.at[:, pl.ds(0, FF_DEV)], load_sem.at[8])
    load_upw = load(up_hbm.at[0], gate_up.at[:, pl.ds(FF_DEV, FF_DEV)], load_sem.at[9])
    load_down = load(down_hbm.at[0], down, load_sem.at[10])

    keys_new[...] = jnp.zeros_like(keys_new)
    keys_new[pl.ds(0, ROWS), :] = new_latent[...]
    twice = (iota((ROPE, 128), 1) % ROPE == iota((ROPE, 128), 0)).astype(BF16)
    rot_new[...] = jnp.zeros_like(rot_new)
    rot_new[pl.ds(0, ROWS), :] = dot(new_rotary[...], twice).astype(BF16)

    expert = x
    weight_row = jnp.sum(
        jnp.where(route_ids[...] == expert, routing_weight[...], 0.0), axis=0, keepdims=True
    )
    chosen_all[...] = jnp.broadcast_to(weight_row, (128, GROUP * ROWS)).T
    for side in range(2):
        for place in range(GROUP // 2):
            source = (place * 2 + (core + side) % 2) * ROWS
            chosen[pl.ds((side * 16 + place) * ROWS, ROWS), :] = chosen_all[
                pl.ds(pl.multiple_of(source, ROWS), ROWS), :
            ]

    row_to = iota((256, 256), 0)
    row_from = iota((256, 256), 1)
    permute = (
        row_from == (row_to % 64) // TB * ROWS + row_to // 64 * TB + row_to % TB
    ).astype(BF16)
    low = iota((ROWS, 128), 1) < ROPE
    load_query.wait()
    load_rot.wait()
    for g in range(8):
        pieces, rot_pieces = [], []
        for h in range(g * 16, g * 16 + 16):
            pieces.append(query[:, pl.ds(h * KVL, KVL)])
            pair = query_rot[:, pl.ds(h // 2 * 128, 128)]
            keep = low if h % 2 == 0 else jnp.logical_not(low)
            rot_pieces.append(jnp.where(keep, pair, jnp.zeros_like(pair)))
        moved = dot(permute, jnp.concatenate(pieces, axis=0)).astype(BF16)
        moved_rot = dot(permute, jnp.concatenate(rot_pieces, axis=0)).astype(BF16)
        for b in range(SEQ):
            query_seq[b, pl.ds(g * 64, 64), :] = moved[b * 64 : b * 64 + 64]
            rot_seq[b, pl.ds(g * 64, 64), :] = moved_rot[b * 64 : b * 64 + 64]

    pl.semaphore_wait(barrier, GROUP - 1 + (2 if sections > 1 else 0))

    scale = (VDIM + ROPE) ** -0.5
    tile = 256

    @pl.loop(0, SEQ)
    def _(b):
        pltpu.make_async_copy(latent_hbm.at[b], latent.at[b], seq_sem.at[0, b]).wait()
        pltpu.make_async_copy(rotary_hbm.at[b], rotary.at[b], seq_sem.at[1, b]).wait()
        keys = latent[b]
        rot_keys = jnp.concatenate([rotary[b], rotary[b]], axis=0)
        length = cache_len[b]
        for part in range(TB * HEADS // tile):
            rows = pl.ds(part * tile, tile)
            q = query_seq[b, rows, :]
            q_rot = rot_seq[b, rows, :]
            s = (dot_t(q, keys) + dot(q_rot, rot_keys)) * scale
            s_new = (dot_t(q, keys_new[...]) + dot_t(q_rot, rot_new[...])) * scale
            s = jnp.where(iota((tile, CACHE), 1) < length, s, -1e30)
            col = iota((tile, 128), 1)
            seen = jnp.logical_and(col // TB == b, col % TB <= iota((tile, 128), 0) % TB)
            s_new = jnp.where(seen, s_new, -1e30)
            top = jnp.maximum(
                jnp.max(s, axis=1, keepdims=True), jnp.max(s_new, axis=1, keepdims=True)
            )
            e = jnp.exp(s - top)
            e_new = jnp.exp(s_new - top)
            total = jnp.sum(e, axis=1, keepdims=True) + jnp.sum(e_new, axis=1, keepdims=True)
            mixed = dot(e.astype(BF16), keys) + dot(e_new.astype(BF16), keys_new[...])
            context[b, rows, :] = (mixed / total).astype(BF16)

        own = pl.ds(pl.multiple_of(me * ROWS, ROWS), ROWS)
        arrived[b, pl.ds(pl.multiple_of(chip * ROWS, ROWS), ROWS), :] = context[b, own, :]

        @pl.loop(1, GROUP)
        def _(offset):
            to = (me + offset) % GROUP
            place = (to + me) % 2 * 16 + chip
            pltpu.make_async_remote_copy(
                src_ref=context.at[b, pl.ds(pl.multiple_of(to * ROWS, ROWS), ROWS), :],
                dst_ref=arrived.at[b, pl.ds(pl.multiple_of(place * ROWS, ROWS), ROWS), :],
                send_sem=context_send.at[b],
                recv_sem=context_recv.at[b],
                device_id={"expert": to},
            ).start()

    for copy in load_up:
        copy.wait()
    sent = pl.ds(0, (GROUP - 1) * ROWS)
    same_head = iota((512, 512), 0) % ROWS // TB == iota((512, 512), 1) // VDIM
    for b in range(SEQ):
        pltpu.make_async_copy(arrived.at[b, sent], arrived.at[b, sent], context_recv.at[b]).wait()
        product = dot(arrived[b], value_up[...])
        diagonal[b] = jnp.where(same_head, product, 0.0).astype(BF16)
    out_row = iota((64, 256), 0)
    in_row = iota((64, 256), 1)
    join = (
        (out_row // ROWS == in_row % 64 // ROWS)
        & (out_row % ROWS // TB == in_row // 64)
        & (out_row % TB == in_row % TB)
    ).astype(BF16)
    for g in range(8):
        group = jnp.concatenate([diagonal[b, pl.ds(g * 64, 64), :] for b in range(SEQ)], axis=0)
        heads[pl.ds(g * 64, 64), :] = dot(join, group).astype(BF16)

    started = []

    def send(source, target, send_sem, recv_sem, to):
        copy = pltpu.make_async_remote_copy(
            src_ref=source, dst_ref=target, send_sem=send_sem, recv_sem=recv_sem, device_id=to
        )
        copy.start()
        started.append(copy)
        return copy

    def reduce_rows(which, partial, finish):
        crossing, first, second = [], [], []

        def cross(k):
            cross_out[which, k] = partial(k, 1).astype(BF16)
            crossing.append(
                send(
                    cross_out.at[which, k],
                    cross_in.at[which, k],
                    sum_send.at[which, k, 0],
                    sum_recv.at[which, k, 0],
                    {"expert": sibling},
                )
            )

        cross(0)
        cross(1)
        for k in range(CHUNKS):
            mine = partial(k, 0)
            crossing[k].wait_recv()
            first_out[which, k] = (
                (mine + cross_in[which, k].astype(F32))
                .astype(BF16)
                .reshape(SIDE, SIDE, ROWS, WIDE)
            )
            copies = []
            for offset in range(1, SIDE):
                if k % 2 == 0:
                    to = (x + offset) % SIDE
                    source = first_out.at[which, k, to]
                    where = device(to, y)
                else:
                    to = (y + offset) % SIDE
                    source = first_out.at[which, k, :, to]
                    where = device(x, to)
                copies.append(
                    send(
                        source,
                        first_in.at[which, k, offset - 1],
                        sum_send.at[which, k, offset],
                        sum_recv.at[which, k, offset],
                        {"expert": where},
                    )
                )
            first.append(copies)
            if k + 2 < CHUNKS:
                cross(k + 2)
        for k in range(CHUNKS):
            for copy in first[k]:
                copy.wait_recv()
            if k % 2 == 0:
                rows = first_out[which, k, x].astype(F32)
            else:
                rows = first_out[which, k, :, y].astype(F32)
            for slot in range(SIDE - 1):
                rows = rows + first_in[which, k, slot].astype(F32)
            second_out[which, k] = rows.astype(BF16)
            copies = []
            for offset in range(1, SIDE):
                if k % 2 == 0:
                    to = (y + offset) % SIDE
                    where = device(x, to)
                else:
                    to = (x + offset) % SIDE
                    where = device(to, y)
                copies.append(
                    send(
                        second_out.at[which, k, to],
                        second_in.at[which, k, offset - 1],
                        sum_send.at[which, k, 3 + offset],
                        sum_recv.at[which, k, 3 + offset],
                        {"expert": where},
                    )
                )
            second.append(copies)
        for k in range(CHUNKS):
            for copy in second[k]:
                copy.wait_recv()
            rows = second_out[which, k, y if k % 2 == 0 else x].astype(F32)
            for slot in range(SIDE - 1):
                rows = rows + second_in[which, k, slot].astype(F32)
            finish(k, rows)

    load_out.wait()
    load_res.wait()

    def projected(k, side):
        return dot(heads[pl.ds(side * HALF, HALF), :], out_weight[:, pl.ds(k * WIDE, WIDE)])

    squares = []

    def add_residual(k, rows):
        rows = rows + residual[:, pl.ds(k * WIDE, WIDE)].astype(F32)
        hidden[k] = rows
        squares.append(jnp.sum(rows * rows, axis=1, keepdims=True))

    reduce_rows(0, projected, add_residual)
    mean = sum(squares[1:], squares[0]) * (1.0 / D)
    factor = lax.rsqrt(mean + 1e-06)

    def block(k, side, across):
        return gathered.at[k, side, across] if k % 2 == 0 else gathered.at[k, side, :, across]

    near, far, handed_over = [], [], []
    for k in range(CHUNKS):
        gathered[k, 0, x, y] = (
            hidden[k] * factor * norm_gain[:, pl.ds(k * WIDE, WIDE)]
        ).astype(BF16)
        copies = []
        for offset in range(1, SIDE):
            where = device(x, (y + offset) % SIDE) if k % 2 == 0 else device((x + offset) % SIDE, y)
            copies.append(
                send(
                    gathered.at[k, 0, x, y],
                    gathered.at[k, 0, x, y],
                    gather_send.at[k, offset - 1],
                    gather_recv.at[k, offset - 1],
                    {"expert": where},
                )
            )
        near.append(copies)

    def to_sibling(k, across, slot):
        return send(
            block(k, 0, across),
            block(k, 1, across),
            gather_send.at[k, 6 + slot],
            gather_recv.at[k, 6 + slot],
            {"expert": sibling},
        )

    for k in range(CHUNKS):
        for copy in near[k]:
            copy.wait_recv()
        here = x if k % 2 == 0 else y
        copies = []
        for offset in range(1, SIDE):
            where = device((x + offset) % SIDE, y) if k % 2 == 0 else device(x, (y + offset) % SIDE)
            copies.append(
                send(
                    block(k, 0, here),
                    block(k, 0, here),
                    gather_send.at[k, 2 + offset],
                    gather_recv.at[k, 2 + offset],
                    {"expert": where},
                )
            )
        far.append(copies)
        handed_over.append([to_sibling(k, here, 0)])

    load_gate.wait()
    load_upw.wait()

    def add_units(k, side):
        rows = gathered[k, side].reshape(HALF, WIDE)
        product = dot(rows, gate_up[pl.ds(k * WIDE, WIDE), :])
        if k == 0:
            hidden_units[side] = product
        else:
            hidden_units[side] = hidden_units[side] + product

    for k in range(CHUNKS):
        here = x if k % 2 == 0 else y
        for offset in range(1, SIDE):
            far[k][offset - 1].wait_recv()
            handed_over[k].append(to_sibling(k, (here + SIDE - offset) % SIDE, offset))
        add_units(k, 0)
    for k in range(CHUNKS):
        for copy in handed_over[k]:
            copy.wait_recv()
        add_units(k, 1)

    def activate(side):
        gate_value = hidden_units[side, :, pl.ds(0, FF_DEV)]
        up_value = hidden_units[side, :, pl.ds(FF_DEV, FF_DEV)]
        activation[side] = (gate_value * jax.nn.sigmoid(gate_value) * up_value).astype(BF16)

    activate(1)
    activate(0)
    load_down.wait()

    def expert_share(k, side):
        product = dot(activation[side], down[:, pl.ds(k * WIDE, WIDE)])
        weight = chosen[pl.ds(side * HALF, HALF), :]
        return product * jnp.concatenate([weight] * (WIDE // 128), axis=1)

    handing = []

    def hand_over(k, rows):
        handed[k] = (hidden[k] + rows).astype(BF16)
        target = out_hbm.at[:, pl.ds(k * WIDE, WIDE)]
        if sections > 1:
            handing.append(
                send(
                    handed.at[k],
                    target,
                    hand_send.at[k],
                    hand_recv.at[k],
                    {"section": (section + 1) % sections},
                )
            )
        else:
            load(handed.at[k], target, hand_recv.at[k]).wait()

    reduce_rows(1, expert_share, hand_over)
    for copy in handing:
        copy.wait_recv()
    for copy in started:
        copy.wait_send()
    for b in range(SEQ):
        pltpu.make_async_copy(context.at[b, sent], context.at[b, sent], context_send.at[b]).wait()


def local(
    residual,
    query_latent,
    query_rotary,
    cache_latent,
    cache_rotary,
    new_latent,
    new_rotary,
    cache_len,
    route_ids,
    routing_weight,
    norm_gain,
    value_up_matrix,
    out_weight,
    gate_weight,
    up_weight,
    down_weight,
):
    sections = lax.axis_size("section")
    far = pl.BlockSpec(memory_space=pl.ANY)
    near = pl.BlockSpec(memory_space=pltpu.VMEM)
    scalar = pl.BlockSpec(memory_space=pltpu.SMEM)
    dma = pltpu.SemaphoreType.DMA
    scratch = [
        pltpu.VMEM((ROWS, D), BF16),
        pltpu.VMEM((ROWS, HEADS * KVL), BF16),
        pltpu.VMEM((ROWS, HEADS * ROPE), BF16),
        pltpu.VMEM((SEQ, CACHE, KVL), BF16),
        pltpu.VMEM((SEQ, ROPE, CACHE), BF16),
        pltpu.VMEM((KVL, 4 * VDIM), BF16),
        pltpu.VMEM((4 * VDIM, D), BF16),
        pltpu.VMEM((D, 2 * FF_DEV), BF16),
        pltpu.VMEM((FF_DEV, D), BF16),
        pltpu.VMEM((SEQ, TB * HEADS, KVL), BF16),
        pltpu.VMEM((SEQ, TB * HEADS, 128), BF16),
        pltpu.VMEM((128, KVL), BF16),
        pltpu.VMEM((128, 128), BF16),
        pltpu.VMEM((SEQ, TB * HEADS, KVL), BF16),
        pltpu.VMEM((SEQ, TB * HEADS, KVL), BF16),
        pltpu.VMEM((SEQ, TB * HEADS, KVL), BF16),
        pltpu.VMEM((GROUP * ROWS, 4 * VDIM), BF16),
        pltpu.VMEM((GROUP * ROWS, 128), F32),
        pltpu.VMEM((GROUP * ROWS, 128), F32),
        pltpu.VMEM((2, CHUNKS, HALF, WIDE), BF16),
        pltpu.VMEM((2, CHUNKS, HALF, WIDE), BF16),
        pltpu.VMEM((2, CHUNKS, SIDE, SIDE, ROWS, WIDE), BF16),
        pltpu.VMEM((2, CHUNKS, SIDE - 1, SIDE, ROWS, WIDE), BF16),
        pltpu.VMEM((2, CHUNKS, SIDE, ROWS, WIDE), BF16),
        pltpu.VMEM((2, CHUNKS, SIDE - 1, ROWS, WIDE), BF16),
        pltpu.VMEM((CHUNKS, ROWS, WIDE), F32),
        pltpu.VMEM((CHUNKS, 2, SIDE, SIDE, ROWS, WIDE), BF16),
        pltpu.VMEM((2, HALF, 2 * FF_DEV), F32),
        pltpu.VMEM((2, HALF, FF_DEV), BF16),
        pltpu.VMEM((CHUNKS, ROWS, WIDE), BF16),
        dma((11,)),
        dma((2, SEQ)),
        dma((SEQ,)),
        dma((SEQ,)),
        dma((2, CHUNKS, 7)),
        dma((2, CHUNKS, 7)),
        dma((CHUNKS, 10)),
        dma((CHUNKS, 10)),
        dma((CHUNKS,)),
        dma((CHUNKS,)),
    ]

    def kernel(*refs):
        layer_kernel(sections, *refs)

    return pl.pallas_call(
        kernel,
        out_shape=jax.ShapeDtypeStruct((ROWS, D), BF16),
        in_specs=[far] * 5 + [near, near, scalar, near, near, near] + [far] * 5,
        out_specs=far,
        scratch_shapes=scratch,
        compiler_params=pltpu.CompilerParams(
            collective_id=0, has_side_effects=True, vmem_limit_bytes=60 * 1024 * 1024
        ),
        name="layer",
    )(
        residual,
        query_latent,
        query_rotary,
        cache_latent,
        cache_rotary,
        new_latent,
        new_rotary.T,
        cache_len,
        route_ids.T,
        routing_weight.T,
        norm_gain,
        value_up_matrix,
        out_weight,
        gate_weight,
        up_weight,
        down_weight,
    )


def solution(mesh):
    rows = P(("section", "expert"), None)
    placed = (
        rows,
        rows,
        rows,
        P(("section", "expert"), None, None),
        P(("section", "expert"), None, None),
        rows,
        P(None, ("section", "expert")),
        P(("section", "expert")),
        P("section", None),
        P("section", None),
        P("section", None),
        P("section", "expert", None, None),
        P("section", "expert", None),
        P("section", None, "expert"),
        P("section", None, "expert"),
        P("section", "expert", None),
    )
    return jax.shard_map(local, mesh=mesh, in_specs=placed, out_specs=rows, check_vma=False)
```

time: 307 us -> 104 us (0.34)
  waiting for transfers between devices: 145 us -> 0 us
  Pallas kernels: 0 us -> 102 us
  blocking collectives: 83.7 us -> 0 us
  local copies, waits for them, and re-layouts: 26.8 us -> 1.55 us
  matrix products: 24.6 us -> 0 us
  between operations: 13.6 us -> 0.01 us
  starting transfers between devices: 7.34 us -> 0 us
  other arithmetic: 5.32 us -> 0 us
    pallas_call x0 -> x1, Pallas kernels: none -> 102 us  [local(): pl.pallas_call(kernel, out_shape=jax.ShapeDtypeStruct((ROWS, D), BF16), i...]
    reduce_scatter x1 -> x0, waiting for transfers between devices: 95 us -> none  [local(): lax.psum_scatter(jnp.dot(flat_heads, out_weight[0], preferred_element_typ...]
    all_to_all x2 -> x0, blocking collectives: 83.7 us -> none  [the longest x1 49.6 us: local(): lax.all_to_all(outgoing, 'expert', split_axis=0, concat_axis=0, tiled=True)]
    all_to_all x1 -> x0, waiting for transfers between devices: 45.8 us -> none  [local(): lax.all_to_all(partial_value.astype(jnp.bfloat16), 'expert', split_axis=0...]
    dot_general x12 -> x0, matrix products: 24.6 us -> none  [the longest x1 7.44 us: attend_latent_heads(): jnp.dot(probability, keys_all, preferred_element_type=jnp.float32)]
    reshape x7 -> x0, local copies, waits for them, and re-layouts: 8.52 us -> none  [the longest x1 5.37 us: local(): flat_in = incoming.reshape(-1, model_width)]
    unnamed x32 -> x1, local copies, waits for them, and re-layouts: 8.06 us -> 1.55 us
    all_to_all x1 -> x0, starting transfers between devices: 5.69 us -> none  [local(): lax.all_to_all(partial_value.astype(jnp.bfloat16), 'expert', split_axis=0...]
  transfers between devices with their start and end apart: 3 -> 0, of which waited for: 3 -> 0; matrix products, arithmetic and copies ran while one was open for 1% -> 0% of each run, Pallas kernels for 0% -> 0%
where the time goes in v1:
time: 104 us; the launch traced here: 103 us
  Pallas kernels  102 us (98%)
  local copies, waits for them, and re-layouts  1.55 us (1%)
    pallas_call x1, Pallas kernels, local(): pl.pallas_call(kernel, out_shape=jax.ShapeDtypeStruct((ROWS, D), BF16), i...  102 us

profile of v1, /device:TPU:8, one launch (start us, length us, event | category | flops | bytes accessed | tf_op | source)
XLA Modules:
  0.0 103.1 jit_solution(6277145022736322469)
XLA Ops:
  0.0 101.6 %layer.1 = bf16[16,3584]{1,0:T(8,128)(2,1)} custom-call(bf16[16,3584]{1,0:T(8,128)(2,1)} %refs_0_.1, bf16[16,65536]{1,0:T(8,128)(2,1)} %refs_1_.1, bf16[16,8192]{1,0:T(8,128)(2,1)} %refs_2_.1, bf16[4,512,512]{2,1,0:T(8,128)(2,1)} %refs_3_.1, bf16[4,64,512]{2,1,0:T(8,128)(2,1)} %refs_4_.1, bf16[16,512]{1,0:T(8,128)(2,1)} %refs_5_.1, bf16[16,64]{1,0:T(8,128)(2,1)} %bitcast.3, ...), custom_call_target="tpu_custom_call" | custom-call | tf_op jit(solution)/shard_map/layer/pallas_call | solution.py:541
  101.6 1.6 %copy.18 = bf16[16,3584]{1,0:T(8,128)(2,1)} copy(bf16[16,3584]{1,0:T(8,128)(2,1)} %layer.1) | data formatting | bytes 229376

commit v2 on v1

v2 whole, which is shorter than its diff:
```python
import jax
import jax.numpy as jnp
from jax import lax
from jax.experimental import pallas as pl
from jax.experimental.pallas import tpu as pltpu
from jax.sharding import PartitionSpec as P

D = 3584
KVL = 512
ROPE = 64
VDIM = 128
HEADS = 128
TB = 4
SEQ = 4
ROWS = 16
CACHE = 512
FF_DEV = 256
SIDE = 4
GROUP = 32
BATCHES = 2
PARTS = 2
CHUNKS = BATCHES * PARTS
WIDE = D // 2 // PARTS
HALF = GROUP * ROWS // 2
SHORT = ROWS // BATCHES

BF16 = jnp.bfloat16
F32 = jnp.float32


def dot(a, b):
    return lax.dot_general(a, b, (((1,), (0,)), ((), ())), preferred_element_type=F32)


def dot_t(a, b):
    return lax.dot_general(a, b, (((1,), (1,)), ((), ())), preferred_element_type=F32)


def iota(shape, dim):
    return lax.broadcasted_iota(jnp.int32, shape, dim)


def layer_kernel(
    sections,
    residual_hbm,
    query_hbm,
    query_rot_hbm,
    latent_hbm,
    rotary_hbm,
    new_latent,
    new_rotary,
    cache_len,
    route_ids,
    routing_weight,
    norm_gain,
    value_up_hbm,
    out_weight_hbm,
    gate_hbm,
    up_hbm,
    down_hbm,
    out_hbm,
    residual,
    query,
    query_rot,
    latent,
    rotary,
    value_up,
    out_weight,
    gate_up,
    down,
    query_seq,
    rot_seq,
    keys_new,
    rot_new,
    context,
    arrived,
    diagonal,
    heads,
    chosen_all,
    chosen,
    cross_out,
    cross_in,
    first_out,
    first_in,
    second_out,
    second_in,
    hidden,
    gathered,
    hidden_units,
    activation,
    mixed_rows,
    handed,
    load_sem,
    context_send,
    context_recv,
    sum_send,
    sum_recv,
    gather_send,
    near_recv,
    far_recv,
    over_recv,
    hand_sem,
):
    section = lax.axis_index("section")
    me = lax.axis_index("expert")
    core = me % 2
    chip = me // 2
    x = chip // SIDE
    y = chip % SIDE
    sibling = chip * 2 + 1 - core

    def device(chip_x, chip_y):
        return (chip_x * SIDE + chip_y) * 2 + core

    barrier = pltpu.get_barrier_semaphore()

    @pl.loop(1, GROUP)
    def _(offset):
        pl.semaphore_signal(barrier, inc=1, device_id={"expert": (me + offset) % GROUP})

    if sections > 1:
        pl.semaphore_signal(barrier, inc=1, device_id={"section": (section + 1) % sections})
        pl.semaphore_signal(
            barrier, inc=1, device_id={"section": (section + sections - 1) % sections}
        )

    def load(source, target, sem):
        copy = pltpu.make_async_copy(source, target, sem)
        copy.start()
        return copy

    load_query = load(query_hbm, query, load_sem.at[0])
    load_rot = load(query_rot_hbm, query_rot, load_sem.at[1])
    load_latent = load(latent_hbm, latent, load_sem.at[2])
    load_rotary = load(rotary_hbm, rotary, load_sem.at[3])
    for j in range(4):
        load(value_up_hbm.at[0, j], value_up.at[:, pl.ds(j * VDIM, VDIM)], load_sem.at[4])
    load_out = load(out_weight_hbm.at[0], out_weight, load_sem.at[5])
    load_res = load(residual_hbm, residual, load_sem.at[6])
    load(gate_hbm.at[0], gate_up.at[:, pl.ds(0, FF_DEV)], load_sem.at[7])
    load(up_hbm.at[0], gate_up.at[:, pl.ds(FF_DEV, FF_DEV)], load_sem.at[7])
    load_down = load(down_hbm.at[0], down, load_sem.at[8])

    def settle(like, sem):
        pltpu.make_async_copy(like, like, sem).wait()

    keys_new[...] = jnp.zeros_like(keys_new)
    keys_new[pl.ds(0, ROWS), :] = new_latent[...]
    twice = (iota((ROPE, 128), 1) % ROPE == iota((ROPE, 128), 0)).astype(BF16)
    rot_new[...] = jnp.zeros_like(rot_new)
    rot_new[pl.ds(0, ROWS), :] = dot(new_rotary[...], twice).astype(BF16)

    expert = x
    weight_row = jnp.sum(
        jnp.where(route_ids[...] == expert, routing_weight[...], 0.0), axis=0, keepdims=True
    )
    chosen_all[...] = jnp.broadcast_to(weight_row, (128, GROUP * ROWS)).T
    for side in range(2):
        for place in range(GROUP // 2):
            source = (place * 2 + (core + side) % 2) * ROWS
            chosen[pl.ds((side * 16 + place) * ROWS, ROWS), :] = chosen_all[
                pl.ds(pl.multiple_of(source, ROWS), ROWS), :
            ]

    row_to = iota((256, 256), 0)
    row_from = iota((256, 256), 1)
    permute = (
        row_from == (row_to % 64) // TB * ROWS + row_to // 64 * TB + row_to % TB
    ).astype(BF16)
    low = iota((ROWS, 128), 1) < ROPE
    load_query.wait()
    load_rot.wait()
    for g in range(8):
        pieces, rot_pieces = [], []
        for h in range(g * 16, g * 16 + 16):
            pieces.append(query[:, pl.ds(h * KVL, KVL)])
            pair = query_rot[:, pl.ds(h // 2 * 128, 128)]
            keep = low if h % 2 == 0 else jnp.logical_not(low)
            rot_pieces.append(jnp.where(keep, pair, jnp.zeros_like(pair)))
        moved = dot(permute, jnp.concatenate(pieces, axis=0)).astype(BF16)
        moved_rot = dot(permute, jnp.concatenate(rot_pieces, axis=0)).astype(BF16)
        for b in range(SEQ):
            query_seq[b, pl.ds(g * 64, 64), :] = moved[b * 64 : b * 64 + 64]
            rot_seq[b, pl.ds(g * 64, 64), :] = moved_rot[b * 64 : b * 64 + 64]

    scale = (VDIM + ROPE) ** -0.5
    tile = 256

    def attend(b):
        keys = latent[b]
        rot_keys = jnp.concatenate([rotary[b], rotary[b]], axis=0)
        length = cache_len[b]
        for part in range(TB * HEADS // tile):
            rows = pl.ds(part * tile, tile)
            q = query_seq[b, rows, :]
            q_rot = rot_seq[b, rows, :]
            s = (dot_t(q, keys) + dot(q_rot, rot_keys)) * scale
            s_new = (dot_t(q, keys_new[...]) + dot_t(q_rot, rot_new[...])) * scale
            s = jnp.where(iota((tile, CACHE), 1) < length, s, -1e30)
            col = iota((tile, 128), 1)
            seen = jnp.logical_and(col // TB == b, col % TB <= iota((tile, 128), 0) % TB)
            s_new = jnp.where(seen, s_new, -1e30)
            top = jnp.maximum(
                jnp.max(s, axis=1, keepdims=True), jnp.max(s_new, axis=1, keepdims=True)
            )
            e = jnp.exp(s - top)
            e_new = jnp.exp(s_new - top)
            total = jnp.sum(e, axis=1, keepdims=True) + jnp.sum(e_new, axis=1, keepdims=True)
            mixed = dot(e.astype(BF16), keys) + dot(e_new.astype(BF16), keys_new[...])
            mixed = (mixed / total).astype(BF16)
            context[b, pl.ds(part * 2, 2)] = mixed.reshape(2, SIDE, 2, ROWS, KVL)

    def send(source, target, send_sem, recv_sem, to):
        pltpu.make_async_remote_copy(
            src_ref=source, dst_ref=target, send_sem=send_sem, recv_sem=recv_sem, device_id=to
        ).start()

    def scatter(b):
        arrived[b, 0, x, y] = context[b, x, y, core]

        @pl.loop(1, GROUP)
        def _(offset):
            to = (me + offset) % GROUP
            send(
                context.at[b, to // 8, to // 2 % SIDE, to % 2],
                arrived.at[b, (to + me) % 2, x, y],
                context_send.at[0],
                context_recv.at[b],
                {"expert": to},
            )

    load_latent.wait()
    load_rotary.wait()
    attend(0)
    pl.semaphore_wait(barrier, GROUP - 1 + (2 if sections > 1 else 0))
    scatter(0)

    @pl.loop(1, SEQ)
    def _(b):
        attend(b)
        scatter(b)

    def columns(c, piece):
        return pl.ds((piece * PARTS + c % PARTS) * WIDE, WIDE)

    def stack(upper, lower):
        count = upper.shape[0] // SHORT
        pair = [upper.reshape(count, SHORT, WIDE), lower.reshape(count, SHORT, WIDE)]
        return jnp.concatenate(pair, axis=1)

    def unstack(blocks):
        blocks = blocks.astype(F32)
        rows = blocks.shape[0] * SHORT
        return [
            blocks[:, SHORT * piece : SHORT * piece + SHORT].reshape(rows, WIDE)
            for piece in range(2)
        ]

    sent = pl.ds(0, (GROUP - 1) * ROWS)
    same_head = iota((512, 512), 0) % ROWS // TB == iota((512, 512), 1) // VDIM
    out_row = iota((64, 256), 0)
    in_row = iota((64, 256), 1)
    join = (
        (out_row // SHORT == in_row % 128 // ROWS)
        & (out_row % SHORT // TB == in_row // 128)
        & (out_row % TB == in_row % TB)
    ).astype(BF16)

    def raise_heads(batch):
        pair = range(2 * batch, 2 * batch + 2)
        for b in pair:
            settle(diagonal.at[b, sent], context_recv.at[b])
            product = dot(arrived[b].reshape(TB * HEADS, KVL), value_up[...])
            diagonal[b] = jnp.where(same_head, product, 0.0).astype(BF16)
        for g in range(4):
            group = jnp.concatenate([diagonal[b, pl.ds(g * 128, 128), :] for b in pair], axis=0)
            heads[batch, pl.ds(g * 64, 64), :] = dot(join, group).astype(BF16)

    def cross(which, c, partial):
        cross_out[which, c] = partial(c, 1).astype(BF16).reshape(HALF, WIDE)
        send(
            cross_out.at[which, c],
            cross_in.at[which, c],
            sum_send.at[which, 0],
            sum_recv.at[which, c, 0],
            {"expert": sibling},
        )

    def along_first(which, c, partial):
        mine = partial(c, 0)
        settle(cross_in.at[which, c], sum_recv.at[which, c, 0])
        theirs = cross_in[which, c].reshape(GROUP // 2, ROWS, WIDE).astype(F32)
        first_out[which, c] = (mine + theirs).astype(BF16).reshape(SIDE, SIDE, ROWS, WIDE)
        for half, step in ((0, 1), (1, SIDE - 1)):
            send(
                first_part(which, c, 2, half),
                first_in.at[which, c, 2, pl.ds(half * 2, 2)],
                sum_send.at[which, 1],
                sum_recv.at[which, c, 3],
                {"expert": ahead(c, step)},
            )
        for half, step in ((1, 1), (0, SIDE - 1)):
            to_neighbour(which, c, half, step)

    def line(c):
        return x if c % 2 == 0 else y

    def ahead(c, step):
        to = (line(c) + step) % SIDE
        return device(to, y) if c % 2 == 0 else device(x, to)

    def first_part(which, c, step, half):
        to = (line(c) + step) % SIDE
        pair = pl.ds(half * 2, 2)
        if c % 2 == 0:
            return first_out.at[which, c, to, pair]
        return first_out.at[which, c, pair, to]

    def to_neighbour(which, c, half, step):
        send(
            first_part(which, c, step, half),
            first_in.at[which, c, 0 if step == 1 else 1, pl.ds(half * 2, 2)],
            sum_send.at[which, 1],
            sum_recv.at[which, c, 1],
            {"expert": ahead(c, step)},
        )

    def relay_first(which, c):
        settle(first_in.at[which, c, 2], sum_recv.at[which, c, 3])
        for half, step in ((0, 1), (1, SIDE - 1)):
            part = first_part(which, c, step, half)
            through = first_in[which, c, 2, pl.ds(half * 2, 2)].astype(F32)
            part[...] = (part[...].astype(F32) + through).astype(BF16)
            to_neighbour(which, c, half, step)

    def along_second(which, c):
        settle(first_in.at[which, c, pl.ds(0, 2)], sum_recv.at[which, c, 1])
        if c % 2 == 0:
            rows = first_out[which, c, x].astype(F32)
        else:
            rows = first_out[which, c, :, y].astype(F32)
        for slot in range(2):
            rows = rows + first_in[which, c, slot].astype(F32)
        second_out[which, c] = rows.astype(BF16)
        for offset in range(1, SIDE):
            if c % 2 == 0:
                to = (y + offset) % SIDE
                where = device(x, to)
            else:
                to = (x + offset) % SIDE
                where = device(to, y)
            send(
                second_out.at[which, c, to],
                second_in.at[which, c, offset - 1],
                sum_send.at[which, 2],
                sum_recv.at[which, c, 2],
                {"expert": where},
            )

    def summed(which, c):
        settle(second_in.at[which, c], sum_recv.at[which, c, 2])
        rows = second_out[which, c, y if c % 2 == 0 else x].astype(F32)
        for slot in range(SIDE - 1):
            rows = rows + second_in[which, c, slot].astype(F32)
        return rows

    def chunks(batch):
        return range(batch * PARTS, batch * PARTS + PARTS)

    def projected(c, side):
        rows = heads[c // PARTS, pl.ds(side * HALF // 2, HALF // 2), :]
        return stack(*[dot(rows, out_weight[:, columns(c, piece)]) for piece in range(2)])

    def block(c, side, across):
        return gathered.at[c, side, across] if c % 2 == 0 else gathered.at[c, side, :, across]

    def normalise(batch):
        rows, squares = {}, 0.0
        half = slice(batch * SHORT, batch * SHORT + SHORT)
        for c in chunks(batch):
            left = [residual[:, columns(c, piece)].astype(F32)[half] for piece in range(2)]
            rows[c] = summed(0, c) + jnp.concatenate(left, axis=0)
            hidden[c] = rows[c]
            square = jnp.sum(rows[c] * rows[c], axis=1, keepdims=True)
            squares = squares + square[:SHORT] + square[SHORT:]
        factor = lax.rsqrt(squares * (1.0 / D) + 1e-06)
        factor = jnp.concatenate([factor, factor], axis=0)
        for c in chunks(batch):
            gain = jnp.concatenate(
                [
                    jnp.broadcast_to(norm_gain[:, columns(c, piece)], (SHORT, WIDE))
                    for piece in range(2)
                ],
                axis=0,
            )
            gathered[c, 0, x, y] = (rows[c] * factor * gain).astype(BF16)
            for offset in range(1, SIDE):
                to = (y if c % 2 == 0 else x) + offset
                send(
                    gathered.at[c, 0, x, y],
                    gathered.at[c, 0, x, y],
                    gather_send.at[0],
                    near_recv.at[c],
                    {"expert": device(x, to % SIDE) if c % 2 == 0 else device(to % SIDE, y)},
                )

    def to_sibling(c, across):
        send(
            block(c, 0, across),
            block(c, 1, across),
            gather_send.at[2],
            over_recv.at[c],
            {"expert": sibling},
        )

    def spread(c):
        settle(second_in.at[0, c], near_recv.at[c])
        here = line(c)
        for slot, step in enumerate(range(1, SIDE)):
            send(
                block(c, 0, here),
                block(c, 0, here),
                gather_send.at[1],
                far_recv.at[c, slot],
                {"expert": ahead(c, step)},
            )
        to_sibling(c, here)

    def add_units(c, side):
        pieces = unstack(gathered[c, side].reshape(GROUP // 2, ROWS, WIDE))
        product = 0.0
        for piece in range(2):
            product = product + dot(pieces[piece].astype(BF16), gate_up[columns(c, piece), :])
        if c % PARTS == 0:
            hidden_units[c // PARTS, side] = product
        else:
            hidden_units[c // PARTS, side] = hidden_units[c // PARTS, side] + product

    def pass_on(c):
        here = line(c)
        for step in range(1, SIDE):
            settle(block(c, 0, here), far_recv.at[c, step - 1])
            to_sibling(c, (here + SIDE - step) % SIDE)
        add_units(c, 0)

    def take_over(c):
        settle(gathered.at[c, 1], over_recv.at[c])
        add_units(c, 1)

    def activate(batch, side):
        gate_value = hidden_units[batch, side, :, pl.ds(0, FF_DEV)]
        up_value = hidden_units[batch, side, :, pl.ds(FF_DEV, FF_DEV)]
        activation[batch, side] = (
            gate_value * jax.nn.sigmoid(gate_value) * up_value
        ).astype(BF16)

    def expert_share(c, side):
        batch = c // PARTS
        weight = chosen[pl.ds(side * HALF, HALF), :].reshape(GROUP // 2, ROWS, 128)
        weight = weight[:, batch * SHORT : batch * SHORT + SHORT].reshape(HALF // 2, 128)
        weight = jnp.concatenate([weight] * (WIDE // 128), axis=1)
        rows = activation[batch, side]
        return stack(*[dot(rows, down[:, columns(c, piece)]) * weight for piece in range(2)])

    def finish(c):
        rows = hidden[c] + summed(1, c)
        if c // PARTS == 0:
            mixed_rows[c] = rows
            return
        before = mixed_rows[c % PARTS]
        for piece in range(2):
            half = slice(piece * SHORT, piece * SHORT + SHORT)
            slot = c % PARTS * 2 + piece
            handed[slot] = jnp.concatenate([before[half], rows[half]], axis=0).astype(BF16)
            target = out_hbm.at[:, columns(c, piece)]
            if sections > 1:
                send(
                    handed.at[slot],
                    target,
                    hand_sem.at[0],
                    hand_sem.at[1],
                    {"section": (section + 1) % sections},
                )
            else:
                load(handed.at[slot], target, hand_sem.at[0]).wait()

    settle(value_up, load_sem.at[4])

    def stage_heads(batch):
        raise_heads(batch)
        if batch == 0:
            load_out.wait()
        for c in chunks(batch):
            cross(0, c, projected)

    def stage_first(batch):
        for c in chunks(batch):
            along_first(0, c, projected)

    def stage_relay(batch):
        for c in chunks(batch):
            relay_first(0, c)

    def stage_second(batch):
        for c in chunks(batch):
            along_second(0, c)

    def stage_norm(batch):
        if batch == 0:
            load_res.wait()
        normalise(batch)

    def stage_spread(batch):
        for c in chunks(batch):
            spread(c)

    def stage_pass(batch):
        if batch == 0:
            settle(gate_up, load_sem.at[7])
        for c in chunks(batch):
            pass_on(c)

    def stage_units(batch):
        for c in chunks(batch):
            take_over(c)
        if batch == 0:
            load_down.wait()
        activate(batch, 1)
        for c in chunks(batch):
            cross(1, c, expert_share)

    def stage_shares(batch):
        activate(batch, 0)
        for c in chunks(batch):
            along_first(1, c, expert_share)

    def stage_through(batch):
        for c in chunks(batch):
            relay_first(1, c)

    def stage_last(batch):
        for c in chunks(batch):
            along_second(1, c)

    def stage_finish(batch):
        for c in chunks(batch):
            finish(c)

    stage_heads(0)
    stage_first(0)
    stage_heads(1)
    stage_relay(0)
    stage_first(1)
    stage_second(0)
    stage_relay(1)
    stage_norm(0)
    stage_second(1)
    stage_spread(0)
    stage_norm(1)
    stage_spread(1)
    stage_pass(0)
    stage_units(0)
    stage_shares(0)
    stage_pass(1)
    stage_units(1)
    stage_through(0)
    stage_shares(1)
    stage_last(0)
    stage_through(1)
    stage_finish(0)
    stage_last(1)
    stage_finish(1)

    settle(diagonal.at[:, sent], context_send.at[0])
    for which in range(2):
        settle(cross_out.at[which], sum_send.at[which, 0])
        settle(first_in.at[which], sum_send.at[which, 1])
        settle(second_in.at[which], sum_send.at[which, 2])
    settle(second_in.at[0], gather_send.at[0])
    settle(first_in.at[0], gather_send.at[1])
    settle(gathered.at[:, 0], gather_send.at[2])
    if sections > 1:
        settle(handed, hand_sem.at[0])
        settle(handed, hand_sem.at[1])


def local(
    residual,
    query_latent,
    query_rotary,
    cache_latent,
    cache_rotary,
    new_latent,
    new_rotary,
    cache_len,
    route_ids,
    routing_weight,
    norm_gain,
    value_up_matrix,
    out_weight,
    gate_weight,
    up_weight,
    down_weight,
):
    sections = lax.axis_size("section")
    far = pl.BlockSpec(memory_space=pl.ANY)
    near = pl.BlockSpec(memory_space=pltpu.VMEM)
    scalar = pl.BlockSpec(memory_space=pltpu.SMEM)
    dma = pltpu.SemaphoreType.DMA
    scratch = [
        pltpu.VMEM((ROWS, D), BF16),
        pltpu.VMEM((ROWS, HEADS * KVL), BF16),
        pltpu.VMEM((ROWS, HEADS * ROPE), BF16),
        pltpu.VMEM((SEQ, CACHE, KVL), BF16),
        pltpu.VMEM((SEQ, ROPE, CACHE), BF16),
        pltpu.VMEM((KVL, 4 * VDIM), BF16),
        pltpu.VMEM((4 * VDIM, D), BF16),
        pltpu.VMEM((D, 2 * FF_DEV), BF16),
        pltpu.VMEM((FF_DEV, D), BF16),
        pltpu.VMEM((SEQ, TB * HEADS, KVL), BF16),
        pltpu.VMEM((SEQ, TB * HEADS, 128), BF16),
        pltpu.VMEM((128, KVL), BF16),
        pltpu.VMEM((128, 128), BF16),
        pltpu.VMEM((SEQ, SIDE, SIDE, 2, ROWS, KVL), BF16),
        pltpu.VMEM((SEQ, 2, SIDE, SIDE, ROWS, KVL), BF16),
        pltpu.VMEM((SEQ, TB * HEADS, KVL), BF16),
        pltpu.VMEM((BATCHES, HALF, 4 * VDIM), BF16),
        pltpu.VMEM((GROUP * ROWS, 128), F32),
        pltpu.VMEM((GROUP * ROWS, 128), F32),
        pltpu.VMEM((2, CHUNKS, HALF, WIDE), BF16),
        pltpu.VMEM((2, CHUNKS, HALF, WIDE), BF16),
        pltpu.VMEM((2, CHUNKS, SIDE, SIDE, ROWS, WIDE), BF16),
        pltpu.VMEM((2, CHUNKS, SIDE - 1, SIDE, ROWS, WIDE), BF16),
        pltpu.VMEM((2, CHUNKS, SIDE, ROWS, WIDE), BF16),
        pltpu.VMEM((2, CHUNKS, SIDE - 1, ROWS, WIDE), BF16),
        pltpu.VMEM((CHUNKS, ROWS, WIDE), F32),
        pltpu.VMEM((CHUNKS, 2, SIDE, SIDE, ROWS, WIDE), BF16),
        pltpu.VMEM((BATCHES, 2, HALF // 2, 2 * FF_DEV), F32),
        pltpu.VMEM((BATCHES, 2, HALF // 2, FF_DEV), BF16),
        pltpu.VMEM((PARTS, ROWS, WIDE), F32),
        pltpu.VMEM((CHUNKS, ROWS, WIDE), BF16),
        dma((9,)),
        dma((1,)),
        dma((SEQ,)),
        dma((2, 3)),
        dma((2, CHUNKS, 4)),
        dma((3,)),
        dma((CHUNKS,)),
        dma((CHUNKS, SIDE - 1)),
        dma((CHUNKS,)),
        dma((2,)),
    ]

    def kernel(*refs):
        layer_kernel(sections, *refs)

    return pl.pallas_call(
        kernel,
        out_shape=jax.ShapeDtypeStruct((ROWS, D), BF16),
        in_specs=[far] * 5 + [near, near, scalar, near, near, near] + [far] * 5,
        out_specs=far,
        scratch_shapes=scratch,
        compiler_params=pltpu.CompilerParams(
            collective_id=0, has_side_effects=True, vmem_limit_bytes=60 * 1024 * 1024
        ),
        name="layer",
    )(
        residual,
        query_latent,
        query_rotary,
        cache_latent,
        cache_rotary,
        new_latent,
        new_rotary.T,
        cache_len,
        route_ids.T,
        routing_weight.T,
        norm_gain,
        value_up_matrix,
        out_weight,
        gate_weight,
        up_weight,
        down_weight,
    )


def solution(mesh):
    rows = P(("section", "expert"), None)
    placed = (
        rows,
        rows,
        rows,
        P(("section", "expert"), None, None),
        P(("section", "expert"), None, None),
        rows,
        P(None, ("section", "expert")),
        P(("section", "expert")),
        P("section", None),
        P("section", None),
        P("section", None),
        P("section", "expert", None, None),
        P("section", "expert", None),
        P("section", None, "expert"),
        P("section", None, "expert"),
        P("section", "expert", None),
    )
    return jax.shard_map(local, mesh=mesh, in_specs=placed, out_specs=rows, check_vma=False)
```

time: 104 us -> 88.7 us (0.85)
  Pallas kernels: 102 us -> 87 us
    pallas_call x1, Pallas kernels: 102 us -> 87 us  [local(): pl.pallas_call(kernel, out_shape=jax.ShapeDtypeStruct((ROWS, D), BF16), i...]
where the time goes in v2:
time: 88.7 us; the launch traced here: 88.5 us
  Pallas kernels  87 us (98%)
  local copies, waits for them, and re-layouts  1.55 us (2%)
    pallas_call x1, Pallas kernels, local(): pl.pallas_call(kernel, out_shape=jax.ShapeDtypeStruct((ROWS, D), BF16), i...  87 us

profile of v2, /device:TPU:8, one launch (start us, length us, event | category | flops | bytes accessed | tf_op | source)
XLA Modules:
  0.0 88.5 jit_solution(2809054989663994130)
XLA Ops:
  0.0 87.0 %layer.1 = bf16[16,3584]{1,0:T(8,128)(2,1)} custom-call(bf16[16,3584]{1,0:T(8,128)(2,1)} %refs_0_.1, bf16[16,65536]{1,0:T(8,128)(2,1)} %refs_1_.1, bf16[16,8192]{1,0:T(8,128)(2,1)} %refs_2_.1, bf16[4,512,512]{2,1,0:T(8,128)(2,1)} %refs_3_.1, bf16[4,64,512]{2,1,0:T(8,128)(2,1)} %refs_4_.1, bf16[16,512]{1,0:T(8,128)(2,1)} %refs_5_.1, bf16[16,64]{1,0:T(8,128)(2,1)} %bitcast.3, ...), custom_call_target="tpu_custom_call" | custom-call | tf_op jit(solution)/shard_map/layer/pallas_call | solution.py:657
  87.0 1.6 %copy.18 = bf16[16,3584]{1,0:T(8,128)(2,1)} copy(bf16[16,3584]{1,0:T(8,128)(2,1)} %layer.1) | data formatting | bytes 229376

commit v3 on v2

--- a/solution.py
+++ b/solution.py
@@ -18,15 +18,20 @@
 SIDE = 4
 GROUP = 32
 BATCHES = 2
-PARTS = 2
+PARTS = 4
 CHUNKS = BATCHES * PARTS
-WIDE = D // 2 // PARTS
+WIDTHS = (512, 384)
 HALF = GROUP * ROWS // 2
 SHORT = ROWS // BATCHES
 
 BF16 = jnp.bfloat16
 F32 = jnp.float32
 
+FARTHEST_FIRST = sorted(
+    [(i, j, k) for i in range(SIDE) for j in range(SIDE) for k in range(2) if i + j + k],
+    key=lambda step: -min(step[0], SIDE - step[0]) - min(step[1], SIDE - step[1]),
+)
+
 
 def dot(a, b):
     return lax.dot_general(a, b, (((1,), (0,)), ((), ())), preferred_element_type=F32)
@@ -38,6 +43,37 @@
 
 def iota(shape, dim):
     return lax.broadcasted_iota(jnp.int32, shape, dim)
+
+
+def kind(c):
+    return c % PARTS // 2
+
+
+def width(c):
+    return WIDTHS[kind(c)]
+
+
+class Chunked:
+    def __init__(self, pair, place):
+        self.pair, self.place = pair, place
+
+    def find(self, index):
+        index = index if isinstance(index, tuple) else (index,)
+        c = index[self.place]
+        slot = c // PARTS * 2 + c % 2
+        return kind(c), index[: self.place] + (slot,) + index[self.place + 1 :]
+
+    def __getitem__(self, index):
+        which, index = self.find(index)
+        return self.pair[which][index]
+
+    def __setitem__(self, index, value):
+        which, index = self.find(index)
+        self.pair[which][index] = value
+
+    @property
+    def at(self):
+        return Chunked([ref.at for ref in self.pair], self.place)
 
 
 def layer_kernel(
@@ -78,18 +114,28 @@
     heads,
     chosen_all,
     chosen,
-    cross_out,
-    cross_in,
-    first_out,
-    first_in,
-    second_out,
-    second_in,
-    hidden,
-    gathered,
+    cross_out_wide,
+    cross_out_narrow,
+    cross_in_wide,
+    cross_in_narrow,
+    first_out_wide,
+    first_out_narrow,
+    first_in_wide,
+    first_in_narrow,
+    second_out_wide,
+    second_out_narrow,
+    second_in_wide,
+    second_in_narrow,
+    hidden_wide,
+    hidden_narrow,
+    gathered_wide,
+    gathered_narrow,
     hidden_units,
     activation,
-    mixed_rows,
-    handed,
+    mixed_rows_wide,
+    mixed_rows_narrow,
+    handed_wide,
+    handed_narrow,
     load_sem,
     context_send,
     context_recv,
@@ -101,6 +147,16 @@
     over_recv,
     hand_sem,
 ):
+    cross_out = Chunked((cross_out_wide, cross_out_narrow), 1)
+    cross_in = Chunked((cross_in_wide, cross_in_narrow), 1)
+    first_out = Chunked((first_out_wide, first_out_narrow), 1)
+    first_in = Chunked((first_in_wide, first_in_narrow), 1)
+    second_out = Chunked((second_out_wide, second_out_narrow), 1)
+    second_in = Chunked((second_in_wide, second_in_narrow), 1)
+    hidden = Chunked((hidden_wide, hidden_narrow), 0)
+    gathered = Chunked((gathered_wide, gathered_narrow), 0)
+    mixed_rows = Chunked((mixed_rows_wide, mixed_rows_narrow), 0)
+    handed = Chunked((handed_wide, handed_narrow), 0)
     section = lax.axis_index("section")
     me = lax.axis_index("expert")
     core = me % 2
@@ -218,15 +274,14 @@
     def scatter(b):
         arrived[b, 0, x, y] = context[b, x, y, core]
 
-        @pl.loop(1, GROUP)
-        def _(offset):
-            to = (me + offset) % GROUP
+        for step_x, step_y, other in FARTHEST_FIRST:
+            to_x, to_y, there = (x + step_x) % SIDE, (y + step_y) % SIDE, (core + other) % 2
             send(
-                context.at[b, to // 8, to // 2 % SIDE, to % 2],
-                arrived.at[b, (to + me) % 2, x, y],
+                context.at[b, to_x, to_y, there],
+                arrived.at[b, other, x, y],
                 context_send.at[0],
                 context_recv.at[b],
-                {"expert": to},
+                {"expert": (to_x * SIDE + to_y) * 2 + there},
             )
 
     load_latent.wait()
@@ -241,18 +296,19 @@
         scatter(b)
 
     def columns(c, piece):
-        return pl.ds((piece * PARTS + c % PARTS) * WIDE, WIDE)
+        start = piece * (D // 2) + c % 2 * (D // 4) + kind(c) * WIDTHS[0]
+        return pl.ds(start, width(c))
 
     def stack(upper, lower):
         count = upper.shape[0] // SHORT
-        pair = [upper.reshape(count, SHORT, WIDE), lower.reshape(count, SHORT, WIDE)]
+        pair = [part.reshape(count, SHORT, part.shape[1]) for part in (upper, lower)]
         return jnp.concatenate(pair, axis=1)
 
     def unstack(blocks):
         blocks = blocks.astype(F32)
         rows = blocks.shape[0] * SHORT
         return [
-            blocks[:, SHORT * piece : SHORT * piece + SHORT].reshape(rows, WIDE)
+            blocks[:, SHORT * piece : SHORT * piece + SHORT].reshape(rows, blocks.shape[2])
             for piece in range(2)
         ]
 
@@ -277,11 +333,11 @@
             heads[batch, pl.ds(g * 64, 64), :] = dot(join, group).astype(BF16)
 
     def cross(which, c, partial):
-        cross_out[which, c] = partial(c, 1).astype(BF16).reshape(HALF, WIDE)
+        cross_out[which, c] = partial(c, 1).astype(BF16).reshape(HALF, width(c))
         send(
             cross_out.at[which, c],
             cross_in.at[which, c],
-            sum_send.at[which, 0],
+            sum_send.at[which, 0, kind(c)],
             sum_recv.at[which, c, 0],
             {"expert": sibling},
         )
@@ -289,13 +345,13 @@
     def along_first(which, c, partial):
         mine = partial(c, 0)
         settle(cross_in.at[which, c], sum_recv.at[which, c, 0])
-        theirs = cross_in[which, c].reshape(GROUP // 2, ROWS, WIDE).astype(F32)
-        first_out[which, c] = (mine + theirs).astype(BF16).reshape(SIDE, SIDE, ROWS, WIDE)
+        theirs = cross_in[which, c].reshape(GROUP // 2, ROWS, width(c)).astype(F32)
+        first_out[which, c] = (mine + theirs).astype(BF16).reshape(SIDE, SIDE, ROWS, width(c))
         for half, step in ((0, 1), (1, SIDE - 1)):
             send(
                 first_part(which, c, 2, half),
                 first_in.at[which, c, 2, pl.ds(half * 2, 2)],
-                sum_send.at[which, 1],
+                sum_send.at[which, 1, kind(c)],
                 sum_recv.at[which, c, 3],
                 {"expert": ahead(c, step)},
             )
@@ -320,7 +376,7 @@
         send(
             first_part(which, c, step, half),
             first_in.at[which, c, 0 if step == 1 else 1, pl.ds(half * 2, 2)],
-            sum_send.at[which, 1],
+            sum_send.at[which, 1, kind(c)],
             sum_recv.at[which, c, 1],
             {"expert": ahead(c, step)},
         )
@@ -352,7 +408,7 @@
             send(
                 second_out.at[which, c, to],
                 second_in.at[which, c, offset - 1],
-                sum_send.at[which, 2],
+                sum_send.at[which, 2, kind(c)],
                 sum_recv.at[which, c, 2],
                 {"expert": where},
             )
@@ -388,7 +444,7 @@
         for c in chunks(batch):
             gain = jnp.concatenate(
                 [
-                    jnp.broadcast_to(norm_gain[:, columns(c, piece)], (SHORT, WIDE))
+                    jnp.broadcast_to(norm_gain[:, columns(c, piece)], (SHORT, width(c)))
                     for piece in range(2)
                 ],
                 axis=0,
@@ -399,7 +455,7 @@
                 send(
                     gathered.at[c, 0, x, y],
                     gathered.at[c, 0, x, y],
-                    gather_send.at[0],
+                    gather_send.at[0, kind(c)],
                     near_recv.at[c],
                     {"expert": device(x, to % SIDE) if c % 2 == 0 else device(to % SIDE, y)},
                 )
@@ -408,7 +464,7 @@
         send(
             block(c, 0, across),
             block(c, 1, across),
-            gather_send.at[2],
+            gather_send.at[2, kind(c)],
             over_recv.at[c],
             {"expert": sibling},
         )
@@ -420,14 +476,14 @@
             send(
                 block(c, 0, here),
                 block(c, 0, here),
-                gather_send.at[1],
+                gather_send.at[1, kind(c)],
                 far_recv.at[c, slot],
                 {"expert": ahead(c, step)},
             )
         to_sibling(c, here)
 
     def add_units(c, side):
-        pieces = unstack(gathered[c, side].reshape(GROUP // 2, ROWS, WIDE))
+        pieces = unstack(gathered[c, side].reshape(GROUP // 2, ROWS, width(c)))
         product = 0.0
         for piece in range(2):
             product = product + dot(pieces[piece].astype(BF16), gate_up[columns(c, piece), :])
@@ -458,7 +514,7 @@
         batch = c // PARTS
         weight = chosen[pl.ds(side * HALF, HALF), :].reshape(GROUP // 2, ROWS, 128)
         weight = weight[:, batch * SHORT : batch * SHORT + SHORT].reshape(HALF // 2, 128)
-        weight = jnp.concatenate([weight] * (WIDE // 128), axis=1)
+        weight = jnp.concatenate([weight] * (width(c) // 128), axis=1)
         rows = activation[batch, side]
         return stack(*[dot(rows, down[:, columns(c, piece)]) * weight for piece in range(2)])
 
@@ -470,19 +526,18 @@
         before = mixed_rows[c % PARTS]
         for piece in range(2):
             half = slice(piece * SHORT, piece * SHORT + SHORT)
-            slot = c % PARTS * 2 + piece
-            handed[slot] = jnp.concatenate([before[half], rows[half]], axis=0).astype(BF16)
+            handed[c % PARTS, piece] = jnp.concatenate([before[half], rows[half]], axis=0).astype(BF16)
             target = out_hbm.at[:, columns(c, piece)]
             if sections > 1:
                 send(
-                    handed.at[slot],
+                    handed.at[c % PARTS, piece],
                     target,
-                    hand_sem.at[0],
-                    hand_sem.at[1],
+                    hand_sem.at[0, kind(c)],
+                    hand_sem.at[1, kind(c)],
                     {"section": (section + 1) % sections},
                 )
             else:
-                load(handed.at[slot], target, hand_sem.at[0]).wait()
+                load(handed.at[c % PARTS, piece], target, hand_sem.at[0, kind(c)]).wait()
 
     settle(value_up, load_sem.at[4])
 
@@ -557,8 +612,8 @@
     stage_second(1)
     stage_spread(0)
     stage_norm(1)
+    stage_pass(0)
     stage_spread(1)
-    stage_pass(0)
     stage_units(0)
     stage_shares(0)
     stage_pass(1)
@@ -567,21 +622,22 @@
     stage_shares(1)
     stage_last(0)
     stage_through(1)
+    stage_last(1)
     stage_finish(0)
-    stage_last(1)
     stage_finish(1)
 
     settle(diagonal.at[:, sent], context_send.at[0])
-    for which in range(2):
-        settle(cross_out.at[which], sum_send.at[which, 0])
-        settle(first_in.at[which], sum_send.at[which, 1])
-        settle(second_in.at[which], sum_send.at[which, 2])
-    settle(second_in.at[0], gather_send.at[0])
-    settle(first_in.at[0], gather_send.at[1])
-    settle(gathered.at[:, 0], gather_send.at[2])
-    if sections > 1:
-        settle(handed, hand_sem.at[0])
-        settle(handed, hand_sem.at[1])
+    for size in range(2):
+        for which in range(2):
+            settle(cross_out.pair[size].at[which], sum_send.at[which, 0, size])
+            settle(first_in.pair[size].at[which], sum_send.at[which, 1, size])
+            settle(second_in.pair[size].at[which], sum_send.at[which, 2, size])
+        settle(second_in.pair[size].at[0], gather_send.at[0, size])
+        settle(first_in.pair[size].at[0], gather_send.at[1, size])
+        settle(gathered.pair[size].at[:, 0], gather_send.at[2, size])
+        if sections > 1:
+            settle(handed.pair[size], hand_sem.at[0, size])
+            settle(handed.pair[size], hand_sem.at[1, size])
 
 
 def local(
@@ -627,28 +683,38 @@
         pltpu.VMEM((BATCHES, HALF, 4 * VDIM), BF16),
         pltpu.VMEM((GROUP * ROWS, 128), F32),
         pltpu.VMEM((GROUP * ROWS, 128), F32),
-        pltpu.VMEM((2, CHUNKS, HALF, WIDE), BF16),
-        pltpu.VMEM((2, CHUNKS, HALF, WIDE), BF16),
-        pltpu.VMEM((2, CHUNKS, SIDE, SIDE, ROWS, WIDE), BF16),
-        pltpu.VMEM((2, CHUNKS, SIDE - 1, SIDE, ROWS, WIDE), BF16),
-        pltpu.VMEM((2, CHUNKS, SIDE, ROWS, WIDE), BF16),
-        pltpu.VMEM((2, CHUNKS, SIDE - 1, ROWS, WIDE), BF16),
-        pltpu.VMEM((CHUNKS, ROWS, WIDE), F32),
-        pltpu.VMEM((CHUNKS, 2, SIDE, SIDE, ROWS, WIDE), BF16),
+        pltpu.VMEM((2, 2 * BATCHES, HALF, WIDTHS[0]), BF16),
+        pltpu.VMEM((2, 2 * BATCHES, HALF, WIDTHS[1]), BF16),
+        pltpu.VMEM((2, 2 * BATCHES, HALF, WIDTHS[0]), BF16),
+        pltpu.VMEM((2, 2 * BATCHES, HALF, WIDTHS[1]), BF16),
+        pltpu.VMEM((2, 2 * BATCHES, SIDE, SIDE, ROWS, WIDTHS[0]), BF16),
+        pltpu.VMEM((2, 2 * BATCHES, SIDE, SIDE, ROWS, WIDTHS[1]), BF16),
+        pltpu.VMEM((2, 2 * BATCHES, SIDE - 1, SIDE, ROWS, WIDTHS[0]), BF16),
+        pltpu.VMEM((2, 2 * BATCHES, SIDE - 1, SIDE, ROWS, WIDTHS[1]), BF16),
+        pltpu.VMEM((2, 2 * BATCHES, SIDE, ROWS, WIDTHS[0]), BF16),
+        pltpu.VMEM((2, 2 * BATCHES, SIDE, ROWS, WIDTHS[1]), BF16),
+        pltpu.VMEM((2, 2 * BATCHES, SIDE - 1, ROWS, WIDTHS[0]), BF16),
+        pltpu.VMEM((2, 2 * BATCHES, SIDE - 1, ROWS, WIDTHS[1]), BF16),
+        pltpu.VMEM((2 * BATCHES, ROWS, WIDTHS[0]), F32),
+        pltpu.VMEM((2 * BATCHES, ROWS, WIDTHS[1]), F32),
+        pltpu.VMEM((2 * BATCHES, 2, SIDE, SIDE, ROWS, WIDTHS[0]), BF16),
+        pltpu.VMEM((2 * BATCHES, 2, SIDE, SIDE, ROWS, WIDTHS[1]), BF16),
         pltpu.VMEM((BATCHES, 2, HALF // 2, 2 * FF_DEV), F32),
         pltpu.VMEM((BATCHES, 2, HALF // 2, FF_DEV), BF16),
-        pltpu.VMEM((PARTS, ROWS, WIDE), F32),
-        pltpu.VMEM((CHUNKS, ROWS, WIDE), BF16),
+        pltpu.VMEM((2, ROWS, WIDTHS[0]), F32),
+        pltpu.VMEM((2, ROWS, WIDTHS[1]), F32),
+        pltpu.VMEM((2, 2, ROWS, WIDTHS[0]), BF16),
+        pltpu.VMEM((2, 2, ROWS, WIDTHS[1]), BF16),
         dma((9,)),
         dma((1,)),
         dma((SEQ,)),
-        dma((2, 3)),
+        dma((2, 3, 2)),
         dma((2, CHUNKS, 4)),
-        dma((3,)),
+        dma((3, 2)),
         dma((CHUNKS,)),
         dma((CHUNKS, SIDE - 1)),
         dma((CHUNKS,)),
-        dma((2,)),
+        dma((2, 2)),
     ]
 
     def kernel(*refs):

time: 88.7 us -> 86.1 us (0.971)
  Pallas kernels: 87 us -> 84.4 us
    pallas_call x1, Pallas kernels: 87 us -> 84.4 us  [local(): pl.pallas_call(kernel, out_shape=jax.ShapeDtypeStruct((ROWS, D), BF16), i...]
where the time goes in v3:
time: 86.1 us; the launch traced here: 85.9 us
  Pallas kernels  84.4 us (98%)
  local copies, waits for them, and re-layouts  1.55 us (2%)
    pallas_call x1, Pallas kernels, local(): pl.pallas_call(kernel, out_shape=jax.ShapeDtypeStruct((ROWS, D), BF16), i...  84.4 us

profile of v3, /device:TPU:8, one launch (start us, length us, event | category | flops | bytes accessed | tf_op | source)
XLA Modules:
  0.0 85.9 jit_solution(6406516808822394156)
XLA Ops:
  0.0 84.4 %layer.1 = bf16[16,3584]{1,0:T(8,128)(2,1)} custom-call(bf16[16,3584]{1,0:T(8,128)(2,1)} %refs_0_.1, bf16[16,65536]{1,0:T(8,128)(2,1)} %refs_1_.1, bf16[16,8192]{1,0:T(8,128)(2,1)} %refs_2_.1, bf16[4,512,512]{2,1,0:T(8,128)(2,1)} %refs_3_.1, bf16[4,64,512]{2,1,0:T(8,128)(2,1)} %refs_4_.1, bf16[16,512]{1,0:T(8,128)(2,1)} %refs_5_.1, bf16[16,64]{1,0:T(8,128)(2,1)} %bitcast.3, ...), custom_call_target="tpu_custom_call" | custom-call | tf_op jit(solution)/shard_map/layer/pallas_call | solution.py:723
  84.4 1.6 %copy.18 = bf16[16,3584]{1,0:T(8,128)(2,1)} copy(bf16[16,3584]{1,0:T(8,128)(2,1)} %layer.1) | data formatting | bytes 229376

commit v4 on v3

--- a/solution.py
+++ b/solution.py
@@ -472,7 +472,7 @@
     def spread(c):
         settle(second_in.at[0, c], near_recv.at[c])
         here = line(c)
-        for slot, step in enumerate(range(1, SIDE)):
+        for slot, step in ((1, 2), (0, 1), (2, 3)):
             send(
                 block(c, 0, here),
                 block(c, 0, here),
@@ -494,7 +494,7 @@
 
     def pass_on(c):
         here = line(c)
-        for step in range(1, SIDE):
+        for step in (1, 3, 2):
             settle(block(c, 0, here), far_recv.at[c, step - 1])
             to_sibling(c, (here + SIDE - step) % SIDE)
         add_units(c, 0)

time: 86.1 us -> 85.3 us (level)
  no operation moved by 1% of the time
where the time goes in v4:
time: 85.3 us; the launch traced here: 85.2 us
  Pallas kernels  83.6 us (98%)
  local copies, waits for them, and re-layouts  1.55 us (2%)
    pallas_call x1, Pallas kernels, local(): pl.pallas_call(kernel, out_shape=jax.ShapeDtypeStruct((ROWS, D), BF16), i...  83.6 us

profile of v4, /device:TPU:8, one launch (start us, length us, event | category | flops | bytes accessed | tf_op | source)
XLA Modules:
  0.0 85.2 jit_solution(4564216192314353697)
XLA Ops:
  0.0 83.6 %layer.1 = bf16[16,3584]{1,0:T(8,128)(2,1)} custom-call(bf16[16,3584]{1,0:T(8,128)(2,1)} %refs_0_.1, bf16[16,65536]{1,0:T(8,128)(2,1)} %refs_1_.1, bf16[16,8192]{1,0:T(8,128)(2,1)} %refs_2_.1, bf16[4,512,512]{2,1,0:T(8,128)(2,1)} %refs_3_.1, bf16[4,64,512]{2,1,0:T(8,128)(2,1)} %refs_4_.1, bf16[16,512]{1,0:T(8,128)(2,1)} %refs_5_.1, bf16[16,64]{1,0:T(8,128)(2,1)} %bitcast.3, ...), custom_call_target="tpu_custom_call" | custom-call | tf_op jit(solution)/shard_map/layer/pallas_call | solution.py:723
  83.6 1.6 %copy.18 = bf16[16,3584]{1,0:T(8,128)(2,1)} copy(bf16[16,3584]{1,0:T(8,128)(2,1)} %layer.1) | data formatting | bytes 229376
